TPU v7x, 32 devices: a whole 2x2x4 slice. The times are simulated.
32 devices in a mesh: srv: 16 (over z, y, x), head: 2 (over core).
Axes of the slice: x: 2, y: 2, z: 4, core: 2. Of those that a mesh axis runs over, the one named last changes fastest.
Arguments:
- tokens: bfloat16 [4096, 4096], P(('srv', 'head')), may hold values from -10.5 to 10.5
- doc_ids: int32 [4096], P(('srv', 'head')), may hold values from 0 to 15, never falling along the last dimension, each value on 1 to 512 neighbouring positions
- w_query: bfloat16 [4096, 2048], P(None, 'head'), may hold values from -1 to 1
- w_key: bfloat16 [4096, 512], P(None, 'head'), may hold values from -1.5 to 1.5
- value_weight: bfloat16 [4096, 512], P(None, 'head'), may hold values from -0.09375 to 0.09375
Outputs:
- attended: bfloat16 [4096, 2048], P(('srv', 'head'))
Inputs may be any that keep to these rules, and one draw needn't show every extreme that they name: `doc_ids`: documents are consecutive runs of at most 512 tokens; one has exactly that many.
All inputs are finite; a program needn't handle non-finite values.
Results may differ from a plain program's by a relative error of at most 0.012.
The roundings to bfloat16 on the way count: a program that leaves them out, or rounds other values in their place, can miss the bound.
Values may be sent and summed in bfloat16 or wider, within the bound.
A program may use at most 64 MiB of HBM per device.

v0:
```python
import jax
import jax.numpy as jnp
from jax import lax
from jax.sharding import PartitionSpec as P

QUERY_HEADS = 16
KEY_VALUE_HEADS = 4
HEAD_SIZE = 128
SPAN = 2


def from_behind(x, axis, by):
    devices = lax.axis_size(axis)
    pairs = [(i, i + by) for i in range(devices) if 0 <= i + by < devices]
    return lax.ppermute(x, axis, pairs)


def on_device(tokens, doc_ids, w_query, w_key, value_weight):
    gathered, group_docs = (
        lax.all_gather(tokens, "head", axis=0, tiled=True),
        lax.all_gather(doc_ids, "head", axis=0, tiled=True),
    )
    group_token = gathered.shape[0]
    local_kv = w_key.shape[1] // HEAD_SIZE
    repeat_factor = QUERY_HEADS // KEY_VALUE_HEADS
    query_row_set = jnp.dot(gathered, w_query, preferred_element_type=jnp.float32).astype(
        jnp.bfloat16
    )
    key_matrix_rows = jnp.dot(gathered, w_key, preferred_element_type=jnp.float32).astype(
        jnp.bfloat16
    )
    value_matrix_rows = jnp.dot(gathered, value_weight, preferred_element_type=jnp.float32).astype(
        jnp.bfloat16
    )
    query_matrix = query_row_set.reshape(group_token, local_kv, repeat_factor, HEAD_SIZE)
    group_index = lax.axis_index("srv")
    query_pos = group_index * group_token + jnp.arange(group_token, dtype=jnp.int32)
    logit_scale = 1.0 / HEAD_SIZE**0.5

    def attend(carried, key_block, value_block, doc_block, distance):
        running, totals, accumulated = carried
        key_pos = (group_index - distance) * group_token + jnp.arange(group_token, dtype=jnp.int32)
        allowed = (
            (group_docs[:, None] == doc_block[None, :])
            & (key_pos[None, :] <= query_pos[:, None])
            & (key_pos[None, :] >= 0)
        )
        score_matrix = (
            jnp.einsum(
                "hfwl,afl->fwha",
                query_matrix,
                key_block.reshape(group_token, local_kv, HEAD_SIZE),
                preferred_element_type=jnp.float32,
            )
            * logit_scale
        )
        score_matrix = jnp.where(allowed[None, None], score_matrix, -1e30)
        newmax = jnp.maximum(running, jnp.max(score_matrix, -1))
        factor = jnp.exp(running - newmax)
        exponent = jnp.exp(score_matrix - newmax[..., None])
        totals = totals * factor + jnp.sum(exponent, -1)
        attention_weight = exponent.astype(jnp.bfloat16)
        accumulated = accumulated * factor[..., None] + jnp.einsum(
            "mjwh,hmn->mjwn",
            attention_weight,
            value_block.reshape(group_token, local_kv, HEAD_SIZE),
            preferred_element_type=jnp.float32,
        )
        return (newmax, totals, accumulated)

    carried = (
        jnp.full((local_kv, repeat_factor, group_token), -1e30, jnp.float32),
        jnp.zeros((local_kv, repeat_factor, group_token), jnp.float32),
        jnp.zeros((local_kv, repeat_factor, group_token, HEAD_SIZE), jnp.float32),
    )
    carried = attend(carried, key_matrix_rows, value_matrix_rows, group_docs, 0)
    for distance in range(1, SPAN + 1):
        key_block, value_block, doc_block = from_behind(
            (key_matrix_rows, value_matrix_rows, group_docs), "srv", distance
        )
        carried = attend(carried, key_block, value_block, doc_block, distance)
    running, totals, accumulated = carried
    result = accumulated / totals[..., None]
    result = (
        jnp.transpose(result, (2, 0, 1, 3))
        .reshape(group_token, local_kv * repeat_factor * HEAD_SIZE)
        .astype(jnp.bfloat16)
    )
    return lax.all_to_all(result, "head", split_axis=0, concat_axis=1, tiled=True)


def solution(mesh):
    in_specs = (
        P(("srv", "head"), None),
        P(("srv", "head")),
        P(None, "head"),
        P(None, "head"),
        P(None, "head"),
    )
    out_specs = P(("srv", "head"), None)
    return jax.shard_map(
        on_device, mesh=mesh, in_specs=in_specs, out_specs=out_specs, check_vma=False
    )
```

profile of v0, /device:TPU:0, one launch (start us, length us, event | category | flops | bytes accessed | tf_op | source)
XLA Modules:
  0.0 71.0 jit_solution(744413274337450284)
XLA Ops:
  6.5 0.0 copy-start
  6.5 0.0 all-gather.3.cloned.1.call-start
  6.5 0.7 %all-gather.3.cloned.1.call-update = ((bf16[128,4096]{1,0:T(8,128)(2,1)}), bf16[256,4096]{1,0:T(8,128)(2,1)}) async-update(((), (), s32[]{:S(2)}) %all-gather.3.cloned.1.call-start, bf16[128,4096]{1,0:T(8,128)(2,1)} %param.5) | async-update | bytes 4194328
  7.3 2.1 %all-gather = s32[2,1,128]{2,1,0:T(1,128)S(1)} all-gather(s32[1,1,128]{2,1,0:T(1,128)} %bitcast.138), channel_id=1, replica_groups=mesh['srv'=16,'head'=2] {'head'}, dimensions={0}, use_global_device_ids=true | all-gather | bytes 1536 | tf_op jit(solution)/shard_map/all_gather | solution.py:21
  9.3 4.7 %collective-permute-start.3 = (s32[256]{0:T(256)S(1)}, s32[256]{0:T(256)S(1)}, u32[]{:S(2)}, u32[]{:S(2)}) collective-permute-start(s32[256]{0:T(256)S(1)} %bitcast.135), channel_id=1, source_target_pairs={{0,4},{2,6},{4,8},{6,10},{8,12},{10,14},{12,16},{14,18},{16,20},{1... | collective-permute-start | bytes 3080 | tf_op jit(solution)/shard_map/ppermute | solution.py:15
  14.0 3.4 %collective-permute-start = (s32[256]{0:T(256)S(1)}, s32[256]{0:T(256)S(1)}, u32[]{:S(2)}, u32[]{:S(2)}) collective-permute-start(s32[256]{0:T(256)S(1)} %bitcast.136), channel_id=1, source_target_pairs={{0,2},{2,4},{4,6},{6,8},{8,10},{10,12},{12,14},{14,16},{16,18},{18... | collective-permute-start | bytes 3080 | tf_op jit(solution)/shard_map/ppermute | solution.py:15
  17.5 0.0 collective-permute-done.3
  17.5 1.2 %collective-permute-done = s32[256]{0:T(256)S(1)} collective-permute-done((s32[256]{0:T(256)S(1)}, s32[256]{0:T(256)S(1)}, u32[]{:S(2)}, u32[]{:S(2)}) %collective-permute-start) | collective-permute-done | bytes 1056 | tf_op jit(solution)/shard_map/ppermute | solution.py:15
  18.7 1.1 %and_and_fusion.2 = (pred[256,256]{0,1:T(8,128)(4,1)}, pred[256,256]{0,1:T(8,128)(4,1)S(1)}, pred[256,256]{0,1:T(8,128)(4,1)S(1)}) fusion(s32[256]{0:T(256)S(1)} %iota_add_fusion.2, s32[256]{0:T(256)S(1)} %bitcast.137, pred[256]{0:T(512)(128)(4,1)S(1)} %broadcast_compare_fusion.2, pred[256]{0:T(512)(128)(4,1)S(1)} %broadcast_compare_fusion, ...), kind=kLoop, calls=%fused_computation.43 | loop fusion | flops 786432 | bytes 203520 | tf_op jit(solution)/shard_map/and | solution.py:44
  19.8 2.4 %all-gather.3.cloned.1.call-done = bf16[256,4096]{1,0:T(8,128)(2,1)} async-done(((bf16[128,4096]{1,0:T(8,128)(2,1)}), bf16[256,4096]{1,0:T(8,128)(2,1)}) %all-gather.3.cloned.1.call-update) | async-done | bytes 2097168 | tf_op jit(solution)/shard_map/all_gather | solution.py:20
  22.2 0.0 copy-done
  22.2 0.0 copy-start.1
  22.2 0.0 copy-start.2
  22.2 2.7 %convolution_convert_fusion.2 = bf16[256,256]{0,1:T(8,128)(2,1)S(1)} fusion(bf16[256,4096]{1,0:T(8,128)(2,1)} %all-gather.3.cloned.1.call-done, bf16[4096,256]{1,0:T(8,128)(2,1)S(1)} %copy-done), kind=kOutput, calls=%fused_computation.26 | convolution fusion | flops 536936448 | bytes 4325376 | tf_op jit(solution)/shard_map/dot_general | solution.py:29
  24.9 4.3 %collective-permute-start.4 = (bf16[256,256]{0,1:T(8,128)(2,1)S(1)}, bf16[256,256]{0,1:T(8,128)(2,1)}, u32[]{:S(2)}, u32[]{:S(2)}) collective-permute-start(bf16[256,256]{0,1:T(8,128)(2,1)S(1)} %convolution_convert_fusion.2), channel_id=1, source_target_pairs={{0,4},{2,6},{4,8},{6,10},{8,12},{10,14},{12,16},{14,18},{16,20},{1... | collective-permute-start | bytes 393224 | tf_op jit(solution)/shard_map/ppermute | solution.py:15
  29.2 4.0 %collective-permute-start.1 = (bf16[256,256]{0,1:T(8,128)(2,1)S(1)}, bf16[256,256]{0,1:T(8,128)(2,1)}, u32[]{:S(2)}, u32[]{:S(2)}) collective-permute-start(bf16[256,256]{0,1:T(8,128)(2,1)S(1)} %convolution_convert_fusion.2), channel_id=1, source_target_pairs={{0,2},{2,4},{4,6},{6,8},{8,10},{10,12},{12,14},{14,16},{16,18},{18... | collective-permute-start | bytes 393224 | tf_op jit(solution)/shard_map/ppermute | solution.py:15
  33.2 0.0 copy-done.1
  33.2 0.0 copy-done.2
  33.2 1.0 %convolution_convert_fusion.1 = bf16[256,256]{0,1:T(8,128)(2,1)S(1)} fusion(bf16[256,4096]{1,0:T(8,128)(2,1)S(1)} %copy-done.1, bf16[4096,256]{1,0:T(8,128)(2,1)S(1)} %copy-done.2), kind=kOutput, calls=%fused_computation.25 | convolution fusion | flops 536936448 | bytes 4325376 | tf_op jit(solution)/shard_map/dot_general | solution.py:32
  34.2 2.7 %collective-permute-start.5 = (bf16[256,256]{0,1:T(8,128)(2,1)S(1)}, bf16[256,256]{0,1:T(8,128)(2,1)}, u32[]{:S(2)}, u32[]{:S(2)}) collective-permute-start(bf16[256,256]{0,1:T(8,128)(2,1)S(1)} %convolution_convert_fusion.1), channel_id=1, source_target_pairs={{0,4},{2,6},{4,8},{6,10},{8,12},{10,14},{12,16},{14,18},{16,20},{1... | collective-permute-start | bytes 393224 | tf_op jit(solution)/shard_map/ppermute | solution.py:15
  36.9 4.0 %collective-permute-start.2 = (bf16[256,256]{0,1:T(8,128)(2,1)S(1)}, bf16[256,256]{0,1:T(8,128)(2,1)}, u32[]{:S(2)}, u32[]{:S(2)}) collective-permute-start(bf16[256,256]{0,1:T(8,128)(2,1)S(1)} %convolution_convert_fusion.1), channel_id=1, source_target_pairs={{0,2},{2,4},{4,6},{6,8},{8,10},{10,12},{12,14},{14,16},{16,18},{18... | collective-permute-start | bytes 393224 | tf_op jit(solution)/shard_map/ppermute | solution.py:15
  40.9 5.8 %convolution_convert_fusion = bf16[256,1024]{1,0:T(8,128)(2,1)S(1)} fusion(bf16[256,4096]{1,0:T(8,128)(2,1)S(1)} %copy-done.1, bf16[4096,1024]{1,0:T(8,128)(2,1)} %param.7), kind=kOutput, calls=%fused_computation.23 | convolution fusion | flops 2147745792 | bytes 11010048 | tf_op jit(solution)/shard_map/dot_general | solution.py:26
  46.7 0.4 reshape.313
  47.1 1.4 %fusion.46 = (f32[2,4,256]{2,1,0:T(4,128)S(1)}, f32[2,4,256,256]{2,3,1,0:T(8,128)S(1)}) fusion(bf16[256,2,128,1]{0,2,3,1:T(8,128)(2,1)S(1)} %bitcast.134, bf16[256,2,4,128]{3,2,1,0:T(4,128)(2,1)S(1)} %reshape.313, pred[256,256]{0,1:T(8,128)(4,1)} %get-tuple-element.12), kind=kOutput, calls=%fused_computation.70 | convolution fusion | flops 135788544 | bytes 2826240 | tf_op jit(solution)/shard_map/hfwl,afl->fwha/dot_general | solution.py:49
  48.5 0.0 collective-permute-done.4
  48.5 1.5 %fusion.7 = (f32[2,4,256]{2,1,0:T(4,128)S(1)}, f32[2,256,256,4]{2,1,3,0:T(8,128)S(1)}) fusion(pred[256,256]{0,1:T(8,128)(4,1)S(1)} %get-tuple-element.13, bf16[256,2,128,1]{0,2,3,1:T(8,128)(2,1)} %bitcast.37, bf16[256,2,4,128]{3,2,1,0:T(4,128)(2,1)S(1)} %reshape.313), kind=kOutput, calls=%fused_computation.13 | convolution fusion | flops 135788544 | bytes 2826240 | tf_op jit(solution)/shard_map/hfwl,afl->fwha/dot_general | solution.py:49
  50.0 0.0 collective-permute-done.1
  50.0 1.5 %fusion.6 = (f32[2,4,256]{2,1,0:T(4,128)S(1)}, f32[2,256,256,4]{2,1,3,0:T(8,128)S(1)}) fusion(pred[256,256]{0,1:T(8,128)(4,1)S(1)} %get-tuple-element.14, bf16[256,2,128,1]{0,2,3,1:T(8,128)(2,1)} %bitcast.33, bf16[256,2,4,128]{3,2,1,0:T(4,128)(2,1)S(1)} %reshape.313), kind=kOutput, calls=%fused_computation.12 | convolution fusion | flops 135788544 | bytes 2826240 | tf_op jit(solution)/shard_map/hfwl,afl->fwha/dot_general | solution.py:49
  51.5 0.0 collective-permute-done.5
  51.5 1.6 %convolution_bitcast_fusion = f32[256,2,4,128]{3,0,2,1:T(8,128)S(1)} fusion(bf16[256,2,128,1]{0,2,3,1:T(8,128)(2,1)} %bitcast.39, f32[2,256,256,4]{2,1,3,0:T(8,128)S(1)} %get-tuple-element.16, f32[2,4,256]{2,1,0:T(4,128)S(1)} %get-tuple-element.7, pred[256,256]{0,1:T(8,128)(4,1)S(1)} %get-tuple-element.13), kind=kOutput, calls=%fused_computation.14 | convolution fusion | flops 136314880 | bytes 3350528 | tf_op jit(solution)/shard_map/mjwh,hmn->mjwn/dot_general | solution.py:63
  53.1 0.9 %fusion.2 = (f32[2,4,256]{2,1,0:T(4,128)S(1)}, f32[2,4,256]{2,1,0:T(4,128)S(1)}) fusion(f32[2,256,256,4]{2,1,3,0:T(8,128)S(1)} %get-tuple-element.18, f32[2,4,256]{2,1,0:T(4,128)S(1)} %get-tuple-element.8, pred[256,256]{0,1:T(8,128)(4,1)S(1)} %get-tuple-element.14, f32[2,4,256]{2,1,0:T(4,128)S(1)} %get-tuple-element.7, ...), kind=kLoop, calls=%fused_computation.8 | loop fusion | flops 4190208 | bytes 4358144 | tf_op jit(solution)/shard_map/reduce_sum | solution.py:61
  54.0 0.3 fusion
  54.4 1.4 %fusion.11 = f32[256,2,4,128]{3,0,2,1:T(8,128)S(1)} fusion(bf16[256,2,128,1]{0,2,3,1:T(8,128)(2,1)S(1)} %bitcast.133, f32[2,4,256,256]{2,3,1,0:T(8,128)S(1)} %get-tuple-element.20, f32[2,4,256]{2,1,0:T(4,128)S(1)} %get-tuple-element.11, f32[256,2,4]{0,2,1:T(4,128)S(1)} %get-tuple-element.9, f32[256,2,4]{0,2,1:T(4,128)S(1)} %get-tuple-element.10), kind=kOutput, calls=%fused_computation.20 | convolution fusion | flops 135790592 | bytes 3301376 | tf_op jit(solution)/shard_map/mjwh,hmn->mjwn/dot_general | solution.py:63
  55.8 0.0 collective-permute-done.2
  55.8 2.1 %fusion.14 = bf16[256,2,4,128]{3,0,2,1:T(8,128)(2,1)S(1)} fusion(f32[256,2,4,128]{3,0,2,1:T(8,128)S(1)} %convolution_bitcast_fusion, f32[256,2,4,128]{3,0,2,1:T(8,128)S(1)} %fusion.11, bf16[256,2,128,1]{0,2,3,1:T(8,128)(2,1)} %bitcast.35, f32[2,256,256,4]{2,1,3,0:T(8,128)S(1)} %get-tuple-element.18, f32[2,4,256]{2,1,0:T(4,128)S(1)} %get-tuple-element.8, ...), kind=kOutput, calls=%fused_computation.24 | convolution fusion | flops 137625600 | bytes 4939776 | tf_op jit(solution)/shard_map/mjwh,hmn->mjwn/dot_general | solution.py:63
  57.9 0.4 copy.58
  58.3 0.4 convert_element_type.32
  58.7 4.2 %all_to_all.16 = bf16[2,128,1024]{2,1,0:T(8,128)(2,1)S(1)} all-to-all(bf16[2,128,1024]{2,1,0:T(8,128)(2,1)S(1)} %convert_element_type.32), channel_id=1, replica_groups=mesh['srv'=16,'head'=2] {'head'}, dimensions={0} | all-to-all | bytes 1048576 | tf_op jit(solution)/shard_map/all_to_all | solution.py:89
  62.9 0.3 copy.59
  63.1 1.0 %copy.60 = bf16[128,2048]{1,0:T(8,128)(2,1)} copy(bf16[128,2048]{0,1:T(8,128)(2,1)S(1)} %bitcast.132) | data formatting | bytes 1048576 | tf_op jit(solution)/shard_map/all_to_all | solution.py:89
  (8 shorter events, 0.1 us)
Async XLA Ops:
  6.5 15.7 %copy-start = (bf16[4096,256]{1,0:T(8,128)(2,1)S(1)}, bf16[4096,256]{1,0:T(8,128)(2,1)}, u32[]{:S(2)}) copy-start(bf16[4096,256]{1,0:T(8,128)(2,1)} %param.8) | copy-start | bytes 6291460
  6.5 15.7 %all-gather.3.cloned.1.call-start = ((), (), s32[]{:S(2)}) async-start(), calls=%async_computation.1 | async-start | bytes 3145728 | tf_op jit(solution)/shard_map/all_gather | solution.py:20
  9.3 8.2 %collective-permute-start.3 = (s32[256]{0:T(256)S(1)}, s32[256]{0:T(256)S(1)}, u32[]{:S(2)}, u32[]{:S(2)}) collective-permute-start(s32[256]{0:T(256)S(1)} %bitcast.135), channel_id=1, source_target_pairs={{0,4},{2,6},{4,8},{6,10},{8,12},{10,14},{12,16},{14,18},{16,20},{1... | collective-permute-start | bytes 3080 | tf_op jit(solution)/shard_map/ppermute | solution.py:15
  14.0 4.7 %collective-permute-start = (s32[256]{0:T(256)S(1)}, s32[256]{0:T(256)S(1)}, u32[]{:S(2)}, u32[]{:S(2)}) collective-permute-start(s32[256]{0:T(256)S(1)} %bitcast.136), channel_id=1, source_target_pairs={{0,2},{2,4},{4,6},{6,8},{8,10},{10,12},{12,14},{14,16},{16,18},{18... | collective-permute-start | bytes 3080 | tf_op jit(solution)/shard_map/ppermute | solution.py:15
  22.2 11.0 %copy-start.1 = (bf16[256,4096]{1,0:T(8,128)(2,1)S(1)}, bf16[256,4096]{1,0:T(8,128)(2,1)}, u32[]{:S(2)}) copy-start(bf16[256,4096]{1,0:T(8,128)(2,1)} %all-gather.3.cloned.1.call-done) | copy-start | bytes 6291460
  22.2 11.0 %copy-start.2 = (bf16[4096,256]{1,0:T(8,128)(2,1)S(1)}, bf16[4096,256]{1,0:T(8,128)(2,1)}, u32[]{:S(2)}) copy-start(bf16[4096,256]{1,0:T(8,128)(2,1)} %param.9) | copy-start | bytes 6291460
  24.9 23.6 %collective-permute-start.4 = (bf16[256,256]{0,1:T(8,128)(2,1)S(1)}, bf16[256,256]{0,1:T(8,128)(2,1)}, u32[]{:S(2)}, u32[]{:S(2)}) collective-permute-start(bf16[256,256]{0,1:T(8,128)(2,1)S(1)} %convolution_convert_fusion.2), channel_id=1, source_target_pairs={{0,4},{2,6},{4,8},{6,10},{8,12},{10,14},{12,16},{14,18},{16,20},{1... | collective-permute-start | bytes 393224 | tf_op jit(solution)/shard_map/ppermute | solution.py:15
  29.2 20.8 %collective-permute-start.1 = (bf16[256,256]{0,1:T(8,128)(2,1)S(1)}, bf16[256,256]{0,1:T(8,128)(2,1)}, u32[]{:S(2)}, u32[]{:S(2)}) collective-permute-start(bf16[256,256]{0,1:T(8,128)(2,1)S(1)} %convolution_convert_fusion.2), channel_id=1, source_target_pairs={{0,2},{2,4},{4,6},{6,8},{8,10},{10,12},{12,14},{14,16},{16,18},{18... | collective-permute-start | bytes 393224 | tf_op jit(solution)/shard_map/ppermute | solution.py:15
  34.2 17.3 %collective-permute-start.5 = (bf16[256,256]{0,1:T(8,128)(2,1)S(1)}, bf16[256,256]{0,1:T(8,128)(2,1)}, u32[]{:S(2)}, u32[]{:S(2)}) collective-permute-start(bf16[256,256]{0,1:T(8,128)(2,1)S(1)} %convolution_convert_fusion.1), channel_id=1, source_target_pairs={{0,4},{2,6},{4,8},{6,10},{8,12},{10,14},{12,16},{14,18},{16,20},{1... | collective-permute-start | bytes 393224 | tf_op jit(solution)/shard_map/ppermute | solution.py:15
  36.9 18.8 %collective-permute-start.2 = (bf16[256,256]{0,1:T(8,128)(2,1)S(1)}, bf16[256,256]{0,1:T(8,128)(2,1)}, u32[]{:S(2)}, u32[]{:S(2)}) collective-permute-start(bf16[256,256]{0,1:T(8,128)(2,1)S(1)} %convolution_convert_fusion.1), channel_id=1, source_target_pairs={{0,2},{2,4},{4,6},{6,8},{8,10},{10,12},{12,14},{14,16},{16,18},{18... | collective-permute-start | bytes 393224 | tf_op jit(solution)/shard_map/ppermute | solution.py:15
Sparse Core Ops, SparseCore 0:
  8.9 13.2 all-gather.2
where the time goes:
time: 71.4 us; the launch traced here: 71 us
  starting transfers between devices  23.2 us (32%)
  matrix products  18.9 us (26%)
  between operations  13.6 us (19%)
  blocking collectives  6.21 us (9%)
  waiting for transfers between devices  4.29 us (6%)
  local copies, waits for them, and re-layouts  2.43 us (3%)
  other arithmetic  2.41 us (3%)
    ppermute x6, starting transfers between devices, from_behind(): return lax.ppermute(x, axis, pairs)  23.2 us
    dot_general x1, matrix products, on_device(): jnp.dot(gathered, w_query, preferred_element_type=jnp.float32)  5.77 us
    dot_general x3, matrix products, attend(): jnp.einsum('mjwh,hmn->mjwn', attention_weight, value_block.reshape(group_...  5.16 us
    dot_general x3, matrix products, attend(): jnp.einsum('hfwl,afl->fwha', query_matrix, key_block.reshape(group_token,...  4.31 us
    all_to_all x1, blocking collectives, on_device(): lax.all_to_all(result, 'head', split_axis=0, concat_axis=1, tiled=True)  4.15 us
    dot_general x1, matrix products, on_device(): jnp.dot(gathered, w_key, preferred_element_type=jnp.float32)  2.67 us
    all_gather x1, waiting for transfers between devices, on_device(): lax.all_gather(tokens, 'head', axis=0, tiled=True)  2.39 us
    all_gather x1, blocking collectives, on_device(): lax.all_gather(doc_ids, 'head', axis=0, tiled=True)  2.05 us
  transfers between devices with their start and end apart: 7, of which 2 were waited for; matrix products, arithmetic and copies ran while one was open for 24% of the time, Pallas kernels for 0%

commit v1 on v0

v1 whole, which is shorter than its diff:
```python
import functools
import math

import jax
import jax.numpy as jnp
from jax import lax
from jax.experimental import pallas as pl
from jax.experimental.pallas import tpu as pltpu
from jax.sharding import PartitionSpec as P

HEAD = 128
REPEAT = 4
EXP2_SCALE = math.log2(math.e) / math.sqrt(HEAD)
MASKED = -1e30
MESH = pl.DeviceIdType.MESH


def kernel(
    n,
    tok_hbm,
    doc_hbm,
    wq_hbm,
    wk_hbm,
    wv_hbm,
    out_ref,
    tok,
    wkv,
    wq,
    kv,
    q,
    acc,
    top,
    bias,
    docs,
    stage,
    tok_sem,
    wkv_sem,
    wq_sem,
    doc_sem,
    pair_send,
    pair_recv,
    doc_send,
    doc_recv,
    kv_send,
    kv_recv,
    out_send,
    out_recv,
):
    srv = lax.axis_index("srv")
    head = lax.axis_index("head")
    other = 1 - head
    tok_dev = tok.shape[1]
    kv_heads = wkv.shape[0]
    q_blocks = wq.shape[0]
    even = srv % 2 == 0
    odd = srv % 2 == 1

    def local(src, dst, sem):
        return pltpu.make_async_copy(src, dst, sem)

    own_tok = local(tok_hbm, tok.at[head], tok_sem)
    own_doc = local(doc_hbm, docs.at[head], doc_sem)
    wkv_copies = []
    for c in range(kv_heads):
        cols = pl.ds(c * HEAD, HEAD)
        wkv_copies.append(
            (
                local(wk_hbm.at[:, cols], wkv.at[c, :, pl.ds(0, HEAD)], wkv_sem.at[c, 0]),
                local(wv_hbm.at[:, cols], wkv.at[c, :, pl.ds(HEAD, HEAD)], wkv_sem.at[c, 1]),
            )
        )
    wq_copies = [
        local(wq_hbm.at[:, pl.ds(j * 256, 256)], wq.at[j], wq_sem.at[j]) for j in range(q_blocks)
    ]
    own_tok.start()
    own_doc.start()
    for pair in wkv_copies:
        for copy in pair:
            copy.start()

    barrier = pltpu.get_barrier_semaphore()
    pl.semaphore_signal(barrier, inc=1, device_id=(srv, other), device_id_type=MESH)
    count = jnp.int32(1)
    for by in (-2, -1, 1, 2):
        there = (srv + by >= 0) & (srv + by < n)
        count = count + there.astype(jnp.int32)

        @pl.when(there)
        def _(by=by):
            pl.semaphore_signal(barrier, inc=1, device_id=(srv + by, head), device_id_type=MESH)

    pl.semaphore_wait(barrier, count)

    def remote(src, dst, send, recv, device):
        return pltpu.make_async_remote_copy(
            src_ref=src,
            dst_ref=dst,
            send_sem=send,
            recv_sem=recv,
            device_id=device,
            device_id_type=MESH,
        )

    partner = (srv, other)
    pair_tok = remote(tok_hbm, tok.at[head], pair_send.at[0], pair_recv.at[0], partner)
    pair_doc = remote(doc_hbm, docs.at[head], pair_send.at[1], pair_recv.at[1], partner)
    pair_doc.start()
    pair_tok.start()
    for copy in wq_copies:
        copy.start()

    def doc_copy(by):
        return remote(
            docs.at[pl.ds(0, 2)],
            docs.at[pl.ds(2 * by, 2)],
            doc_send.at[by - 1],
            doc_recv.at[by - 1],
            (srv + by, head),
        )

    halves = (head, other)

    def kv_copy(by, turn, c):
        return remote(
            kv.at[0, c, halves[turn]],
            kv.at[by, c, halves[turn]],
            kv_send.at[by - 1, turn, c],
            kv_recv.at[by - 1, turn, c],
            (srv + by, head),
        )

    def kv_forward(turn, c):
        return remote(
            kv.at[2, c, halves[turn]],
            kv.at[1, c, halves[turn]],
            kv_send.at[0, turn, c],
            kv_recv.at[0, turn, c],
            (srv - 1, head),
        )

    sends_one = even & (srv + 1 < n)
    sends_two = srv + 2 < n
    forwards = odd & (srv >= 2)

    def project_kv(turn, c):
        kv[0, c, halves[turn]] = jnp.dot(
            tok[halves[turn]], wkv[c], preferred_element_type=jnp.float32
        ).astype(jnp.bfloat16)

        @pl.when(sends_two)
        def _():
            kv_copy(2, turn, c).start()

        @pl.when(sends_one)
        def _():
            kv_copy(1, turn, c).start()

    def project_q(turn, j):
        block = jnp.dot(
            tok[halves[turn]], wq[j], preferred_element_type=jnp.float32
        ).astype(jnp.bfloat16)
        q[2 * j, halves[turn]] = block[:, :HEAD]
        q[2 * j + 1, halves[turn]] = block[:, HEAD:]

    def forward(turn, c):
        @pl.when(forwards)
        def _():
            kv_copy(2, turn, c).wait_recv()
            kv_forward(turn, c).start()

    own_tok.wait()
    own_doc.wait()
    for c in range(kv_heads):
        for copy in wkv_copies[c]:
            copy.wait()
        project_kv(0, c)
    pair_doc.wait_recv()
    for by in (1, 2):

        @pl.when(srv + by < n)
        def _(by=by):
            doc_copy(by).start()

    for j in range(q_blocks):
        wq_copies[j].wait()
        project_q(0, j)
    pair_tok.wait_recv()
    for c in range(kv_heads):
        project_kv(1, c)
    for c in range(kv_heads):
        forward(0, c)
    for j in range(q_blocks):
        project_q(1, j)

    def column(part):
        ids = docs[part].astype(jnp.float32)
        return jnp.transpose(jnp.broadcast_to(ids, (HEAD, HEAD)))

    def set_bias(block):
        for r in range(2):
            mine = column(r)
            for s in range(2):
                theirs = docs[2 * block + s].astype(jnp.float32)
                allowed = mine == theirs
                if block == 0:
                    rows = lax.broadcasted_iota(jnp.int32, (HEAD, HEAD), 0) + r * HEAD
                    cols = lax.broadcasted_iota(jnp.int32, (HEAD, HEAD), 1) + s * HEAD
                    allowed = allowed & (cols <= rows)
                bias[block, r, :, s * HEAD : (s + 1) * HEAD] = jnp.where(allowed, 0.0, MASKED)

    ones = jnp.ones((2 * tok_dev, HEAD), jnp.bfloat16)

    def attend(block, c):
        both = kv[block, c].reshape(2 * tok_dev, 2 * HEAD)
        keys = both[:, :HEAD]
        values = jnp.concatenate([both[:, HEAD:], ones], axis=1)
        for g in range(REPEAT):
            h = c * REPEAT + g
            for r in range(2):
                score = lax.dot_general(
                    q[h, r], keys, (((1,), (1,)), ((), ())), preferred_element_type=jnp.float32
                )
                score = score + bias[block, r]
                high = jnp.max(score, axis=1, keepdims=True)
                if block:
                    before = top[h, r][:, :1]
                    high = jnp.maximum(high, before)
                weight = jnp.exp2((score - high) * EXP2_SCALE).astype(jnp.bfloat16)
                part = jnp.dot(weight, values, preferred_element_type=jnp.float32)
                if block:
                    part = part + acc[h, r] * jnp.exp2((before - high) * EXP2_SCALE)
                acc[h, r] = part
                if block != 1:
                    top[h, r] = jnp.broadcast_to(high, (tok_dev, HEAD))

    set_bias(0)
    for c in range(kv_heads):
        attend(0, c)
    for c in range(kv_heads):
        forward(1, c)

    @pl.when(srv >= 2)
    def _():
        doc_copy(2).wait_recv()
        set_bias(2)
        for c in range(kv_heads):

            @pl.when(even)
            def _():
                for turn in range(2):
                    kv_copy(2, turn, c).wait_recv()

            attend(2, c)

    @pl.when(srv >= 1)
    def _():
        doc_copy(1).wait_recv()
        set_bias(1)

    def out_copy(c):
        width = REPEAT * HEAD
        column_of = pl.multiple_of(head * kv_heads * width + c * width, width)
        return remote(
            stage.at[c],
            out_ref.at[:, pl.ds(column_of, width)],
            out_send.at[c],
            out_recv.at[c],
            partner,
        )

    for c in range(kv_heads):

        @pl.when(srv >= 1)
        def _():
            for turn in range(2):
                kv_copy(1, turn, c).wait_recv()
            attend(1, c)

        for g in range(REPEAT):
            h = c * REPEAT + g
            theirs = acc[h, other]
            stage[c, :, g * HEAD : (g + 1) * HEAD] = (theirs[:, :HEAD] / theirs[:, HEAD:]).astype(
                jnp.bfloat16
            )
        out_copy(c).start()
        for g in range(REPEAT):
            h = c * REPEAT + g
            mine = acc[h, head]
            at = pl.multiple_of((head * kv_heads + c) * REPEAT * HEAD + g * HEAD, HEAD)
            out_ref[:, pl.ds(at, HEAD)] = (mine[:, :HEAD] / mine[:, HEAD:]).astype(jnp.bfloat16)

    pair_tok.wait_send()
    pair_doc.wait_send()
    for by in (1, 2):

        @pl.when(srv + by < n)
        def _(by=by):
            doc_copy(by).wait_send()

    for turn in range(2):
        for c in range(kv_heads):

            @pl.when(sends_two)
            def _():
                kv_copy(2, turn, c).wait_send()

            @pl.when(sends_one)
            def _():
                kv_copy(1, turn, c).wait_send()

            @pl.when(forwards)
            def _():
                kv_forward(turn, c).wait_send()

    for c in range(kv_heads):
        out_copy(c).wait()


def on_device(n, tokens, doc_ids, w_query, w_key, value_weight):
    tok_dev, width = tokens.shape
    kv_heads = w_key.shape[1] // HEAD
    heads = w_query.shape[1] // HEAD
    q_blocks = heads // 2
    bf16, f32 = jnp.bfloat16, jnp.float32
    dma = pltpu.SemaphoreType.DMA
    return pl.pallas_call(
        functools.partial(kernel, n),
        out_shape=jax.ShapeDtypeStruct((tok_dev, 2 * heads * HEAD), bf16),
        in_specs=[pl.BlockSpec(memory_space=pl.ANY)] * 5,
        out_specs=pl.BlockSpec(memory_space=pltpu.VMEM),
        scratch_shapes=[
            pltpu.VMEM((2, tok_dev, width), bf16),
            pltpu.VMEM((kv_heads, width, 2 * HEAD), bf16),
            pltpu.VMEM((q_blocks, width, 2 * HEAD), bf16),
            pltpu.VMEM((3, kv_heads, 2, tok_dev, 2 * HEAD), bf16),
            pltpu.VMEM((heads, 2, tok_dev, HEAD), bf16),
            pltpu.VMEM((heads, 2, tok_dev, 2 * HEAD), f32),
            pltpu.VMEM((heads, 2, tok_dev, HEAD), f32),
            pltpu.VMEM((3, 2, tok_dev, 2 * tok_dev), f32),
            pltpu.VMEM((6, 1, tok_dev), jnp.int32),
            pltpu.VMEM((kv_heads, tok_dev, REPEAT * HEAD), bf16),
            dma,
            dma((kv_heads, 2)),
            dma((q_blocks,)),
            dma,
            dma((2,)),
            dma((2,)),
            dma((2,)),
            dma((2,)),
            dma((2, 2, kv_heads)),
            dma((2, 2, kv_heads)),
            dma((kv_heads,)),
            dma((kv_heads,)),
        ],
        compiler_params=pltpu.CompilerParams(
            collective_id=0, has_side_effects=True, vmem_limit_bytes=48 * 1024 * 1024
        ),
    )(tokens, doc_ids.reshape(1, tok_dev), w_query, w_key, value_weight)


def solution(mesh):
    in_specs = (
        P(("srv", "head"), None),
        P(("srv", "head")),
        P(None, "head"),
        P(None, "head"),
        P(None, "head"),
    )
    return jax.shard_map(
        functools.partial(on_device, mesh.shape["srv"]),
        mesh=mesh,
        in_specs=in_specs,
        out_specs=P(("srv", "head"), None),
        check_vma=False,
    )
```

time: 71.4 us -> 26.7 us (0.37)
  the two profiles are of different devices: /device:TPU:0 before, /device:TPU:27 now
where the time goes in v1:
time: 26.7 us; the launch traced here: 26.5 us
  Pallas kernels  20.6 us (77%)
  local copies, waits for them, and re-layouts  5.86 us (22%)
    pallas_call x1, Pallas kernels, on_device(): pl.pallas_call(functools.partial(kernel, n), out_shape=jax.ShapeDtypeStru...  20.6 us
    unnamed x9, local copies, waits for them, and re-layouts  5.86 us

profile of v1, /device:TPU:27, one launch (start us, length us, event | category | flops | bytes accessed | tf_op | source)
XLA Modules:
  0.0 26.5 jit_solution(4194661600777119516)
XLA Ops:
  0.0 0.0 copy-start
  0.0 1.6 %copy-done = bf16[4096,256]{1,0:T(8,128)(2,1)S(1)} copy-done((bf16[4096,256]{1,0:T(8,128)(2,1)S(1)}, bf16[4096,256]{1,0:T(8,128)(2,1)}, u32[]{:S(2)}) %copy-start) | copy-done | bytes 2097176
  1.6 0.0 copy-start.1
  1.6 1.6 %copy-done.1 = bf16[4096,256]{1,0:T(8,128)(2,1)S(1)} copy-done((bf16[4096,256]{1,0:T(8,128)(2,1)S(1)}, bf16[4096,256]{1,0:T(8,128)(2,1)}, u32[]{:S(2)}) %copy-start.1) | copy-done | bytes 2097176
  3.2 0.0 copy-start.2
  3.2 1.2 %copy-done.2 = bf16[128,4096]{1,0:T(8,128)(2,1)S(1)} copy-done((bf16[128,4096]{1,0:T(8,128)(2,1)S(1)}, bf16[128,4096]{1,0:T(8,128)(2,1)}, u32[]{:S(2)}) %copy-start.2) | copy-done | bytes 1048600
  4.4 0.0 copy-start.3
  4.4 0.7 %copy-done.3 = s32[128]{0:T(128)S(1)} copy-done((s32[128]{0:T(128)S(1)}, s32[128]{0:T(128)}, u32[]{:S(2)}) %copy-start.3) | copy-done | bytes 536
  5.1 20.6 %shard_map.55 = bf16[128,2048]{1,0:T(8,128)(2,1)S(1)} custom-call(bf16[128,4096]{1,0:T(8,128)(2,1)S(1)} %copy-done.2, s32[1,128]{1,0:T(1,128)S(1)} %bitcast.1, bf16[4096,1024]{1,0:T(8,128)(2,1)} %wq_hbm.1, bf16[4096,256]{1,0:T(8,128)(2,1)S(1)} %copy-done, bf16[4096,256]{1,0:T(8,128)(2,1)S(1)} %copy-done.1), custom_call_target="tpu_custom_call" | custom-call | tf_op jit(solution)/shard_map/pallas_call | solution.py:326
  25.7 0.8 %copy.7 = bf16[128,2048]{1,0:T(8,128)(2,1)} copy(bf16[128,2048]{1,0:T(8,128)(2,1)S(1)} %shard_map.55) | data formatting | bytes 1048576
Async XLA Ops:
  0.0 1.6 %copy-start = (bf16[4096,256]{1,0:T(8,128)(2,1)S(1)}, bf16[4096,256]{1,0:T(8,128)(2,1)}, u32[]{:S(2)}) copy-start(bf16[4096,256]{1,0:T(8,128)(2,1)} %wk_hbm.1) | copy-start | bytes 6291460
  1.6 1.6 %copy-start.1 = (bf16[4096,256]{1,0:T(8,128)(2,1)S(1)}, bf16[4096,256]{1,0:T(8,128)(2,1)}, u32[]{:S(2)}) copy-start(bf16[4096,256]{1,0:T(8,128)(2,1)} %wv_hbm.1) | copy-start | bytes 6291460
  3.2 1.2 %copy-start.2 = (bf16[128,4096]{1,0:T(8,128)(2,1)S(1)}, bf16[128,4096]{1,0:T(8,128)(2,1)}, u32[]{:S(2)}) copy-start(bf16[128,4096]{1,0:T(8,128)(2,1)} %tok_hbm.1) | copy-start | bytes 3145732
  4.4 0.7 %copy-start.3 = (s32[128]{0:T(128)S(1)}, s32[128]{0:T(128)}, u32[]{:S(2)}) copy-start(s32[128]{0:T(128)} %param.6) | copy-start | bytes 1540

commit v2 on v1

--- a/solution.py
+++ b/solution.py
@@ -77,6 +77,8 @@
     for pair in wkv_copies:
         for copy in pair:
             copy.start()
+    for copy in wq_copies:
+        copy.start()
 
     barrier = pltpu.get_barrier_semaphore()
     pl.semaphore_signal(barrier, inc=1, device_id=(srv, other), device_id_type=MESH)
@@ -106,8 +108,6 @@
     pair_doc = remote(doc_hbm, docs.at[head], pair_send.at[1], pair_recv.at[1], partner)
     pair_doc.start()
     pair_tok.start()
-    for copy in wq_copies:
-        copy.start()
 
     def doc_copy(by):
         return remote(
@@ -155,12 +155,12 @@
         def _():
             kv_copy(1, turn, c).start()
 
-    def project_q(turn, j):
+    def project_q(j):
         block = jnp.dot(
-            tok[halves[turn]], wq[j], preferred_element_type=jnp.float32
+            tok[...].reshape(2 * tok_dev, tok.shape[2]), wq[j], preferred_element_type=jnp.float32
         ).astype(jnp.bfloat16)
-        q[2 * j, halves[turn]] = block[:, :HEAD]
-        q[2 * j + 1, halves[turn]] = block[:, HEAD:]
+        q[2 * j] = block[:, :HEAD]
+        q[2 * j + 1] = block[:, HEAD:]
 
     def forward(turn, c):
         @pl.when(forwards)
@@ -181,16 +181,15 @@
         def _(by=by):
             doc_copy(by).start()
 
+    pair_tok.wait_recv()
+    for c in range(kv_heads):
+        project_kv(1, c)
     for j in range(q_blocks):
+        if j == q_blocks // 2:
+            for c in range(kv_heads):
+                forward(0, c)
         wq_copies[j].wait()
-        project_q(0, j)
-    pair_tok.wait_recv()
-    for c in range(kv_heads):
-        project_kv(1, c)
-    for c in range(kv_heads):
-        forward(0, c)
-    for j in range(q_blocks):
-        project_q(1, j)
+        project_q(j)
 
     def column(part):
         ids = docs[part].astype(jnp.float32)
@@ -206,7 +205,7 @@
                     rows = lax.broadcasted_iota(jnp.int32, (HEAD, HEAD), 0) + r * HEAD
                     cols = lax.broadcasted_iota(jnp.int32, (HEAD, HEAD), 1) + s * HEAD
                     allowed = allowed & (cols <= rows)
-                bias[block, r, :, s * HEAD : (s + 1) * HEAD] = jnp.where(allowed, 0.0, MASKED)
+                bias[block, r * HEAD : (r + 1) * HEAD, s * HEAD : (s + 1) * HEAD] = jnp.where(allowed, 0.0, MASKED)
 
     ones = jnp.ones((2 * tok_dev, HEAD), jnp.bfloat16)
 
@@ -214,24 +213,32 @@
         both = kv[block, c].reshape(2 * tok_dev, 2 * HEAD)
         keys = both[:, :HEAD]
         values = jnp.concatenate([both[:, HEAD:], ones], axis=1)
+
+        def scores(g):
+            return lax.dot_general(
+                q[c * REPEAT + g],
+                keys,
+                (((1,), (1,)), ((), ())),
+                preferred_element_type=jnp.float32,
+            )
+
+        ahead = scores(0)
         for g in range(REPEAT):
             h = c * REPEAT + g
-            for r in range(2):
-                score = lax.dot_general(
-                    q[h, r], keys, (((1,), (1,)), ((), ())), preferred_element_type=jnp.float32
-                )
-                score = score + bias[block, r]
-                high = jnp.max(score, axis=1, keepdims=True)
-                if block:
-                    before = top[h, r][:, :1]
-                    high = jnp.maximum(high, before)
-                weight = jnp.exp2((score - high) * EXP2_SCALE).astype(jnp.bfloat16)
-                part = jnp.dot(weight, values, preferred_element_type=jnp.float32)
-                if block:
-                    part = part + acc[h, r] * jnp.exp2((before - high) * EXP2_SCALE)
-                acc[h, r] = part
-                if block != 1:
-                    top[h, r] = jnp.broadcast_to(high, (tok_dev, HEAD))
+            score = ahead + bias[block]
+            if g + 1 < REPEAT:
+                ahead = scores(g + 1)
+            high = jnp.max(score, axis=1, keepdims=True)
+            if block:
+                before = top[h][:, :1]
+                high = jnp.maximum(high, before)
+            weight = jnp.exp2((score - high) * EXP2_SCALE).astype(jnp.bfloat16)
+            part = jnp.dot(weight, values, preferred_element_type=jnp.float32)
+            if block:
+                part = part + acc[h] * jnp.exp2((before - high) * EXP2_SCALE)
+            acc[h] = part
+            if block != 1:
+                top[h] = jnp.broadcast_to(high, (2 * tok_dev, HEAD))
 
     set_bias(0)
     for c in range(kv_heads):
@@ -278,14 +285,14 @@
 
         for g in range(REPEAT):
             h = c * REPEAT + g
-            theirs = acc[h, other]
+            theirs = acc[h, pl.ds(pl.multiple_of(other * tok_dev, tok_dev), tok_dev)]
             stage[c, :, g * HEAD : (g + 1) * HEAD] = (theirs[:, :HEAD] / theirs[:, HEAD:]).astype(
                 jnp.bfloat16
             )
         out_copy(c).start()
         for g in range(REPEAT):
             h = c * REPEAT + g
-            mine = acc[h, head]
+            mine = acc[h, pl.ds(pl.multiple_of(head * tok_dev, tok_dev), tok_dev)]
             at = pl.multiple_of((head * kv_heads + c) * REPEAT * HEAD + g * HEAD, HEAD)
             out_ref[:, pl.ds(at, HEAD)] = (mine[:, :HEAD] / mine[:, HEAD:]).astype(jnp.bfloat16)
 
@@ -326,17 +333,17 @@
     return pl.pallas_call(
         functools.partial(kernel, n),
         out_shape=jax.ShapeDtypeStruct((tok_dev, 2 * heads * HEAD), bf16),
-        in_specs=[pl.BlockSpec(memory_space=pl.ANY)] * 5,
+        in_specs=[pl.BlockSpec(memory_space=pltpu.HBM)] * 5,
         out_specs=pl.BlockSpec(memory_space=pltpu.VMEM),
         scratch_shapes=[
             pltpu.VMEM((2, tok_dev, width), bf16),
             pltpu.VMEM((kv_heads, width, 2 * HEAD), bf16),
             pltpu.VMEM((q_blocks, width, 2 * HEAD), bf16),
             pltpu.VMEM((3, kv_heads, 2, tok_dev, 2 * HEAD), bf16),
-            pltpu.VMEM((heads, 2, tok_dev, HEAD), bf16),
-            pltpu.VMEM((heads, 2, tok_dev, 2 * HEAD), f32),
-            pltpu.VMEM((heads, 2, tok_dev, HEAD), f32),
-            pltpu.VMEM((3, 2, tok_dev, 2 * tok_dev), f32),
+            pltpu.VMEM((heads, 2 * tok_dev, HEAD), bf16),
+            pltpu.VMEM((heads, 2 * tok_dev, 2 * HEAD), f32),
+            pltpu.VMEM((heads, 2 * tok_dev, HEAD), f32),
+            pltpu.VMEM((3, 2 * tok_dev, 2 * tok_dev), f32),
             pltpu.VMEM((6, 1, tok_dev), jnp.int32),
             pltpu.VMEM((kv_heads, tok_dev, REPEAT * HEAD), bf16),
             dma,
@@ -353,7 +360,7 @@
             dma((kv_heads,)),
         ],
         compiler_params=pltpu.CompilerParams(
-            collective_id=0, has_side_effects=True, vmem_limit_bytes=48 * 1024 * 1024
+            collective_id=0, has_side_effects=True, vmem_limit_bytes=56 * 1024 * 1024
         ),
     )(tokens, doc_ids.reshape(1, tok_dev), w_query, w_key, value_weight)
 

time: 26.7 us -> 26.8 us (level)
  the two profiles are of different devices: /device:TPU:27 before, /device:TPU:17 now
where the time goes in v2:
time: 26.8 us; the launch traced here: 26.5 us
  Pallas kernels  24.6 us (92%)
  local copies, waits for them, and re-layouts  1.88 us (7%)
    pallas_call x1, Pallas kernels, on_device(): pl.pallas_call(functools.partial(kernel, n), out_shape=jax.ShapeDtypeStru...  24.6 us
    unnamed x1, local copies, waits for them, and re-layouts  1.88 us

profile of v2, /device:TPU:17, one launch (start us, length us, event | category | flops | bytes accessed | tf_op | source)
XLA Modules:
  0.0 26.5 jit_solution(13436590094225239626)
XLA Ops:
  0.0 24.6 %shard_map.55 = bf16[128,2048]{1,0:T(8,128)(2,1)} custom-call(bf16[128,4096]{1,0:T(8,128)(2,1)} %tok_hbm.1, s32[1,128]{1,0:T(1,128)} %bitcast.1, bf16[4096,1024]{1,0:T(8,128)(2,1)} %wq_hbm.1, bf16[4096,256]{1,0:T(8,128)(2,1)} %wk_hbm.1, bf16[4096,256]{1,0:T(8,128)(2,1)} %wv_hbm.1), custom_call_target="tpu_custom_call" | custom-call | tf_op jit(solution)/shard_map/pallas_call | solution.py:333
  24.6 1.9 %copy.7 = bf16[128,2048]{1,0:T(8,128)(2,1)} copy(bf16[128,2048]{1,0:T(8,128)(2,1)} %shard_map.55) | data formatting | bytes 1048576

commit v3 on v2

--- a/solution.py
+++ b/solution.py
@@ -12,6 +12,7 @@
 REPEAT = 4
 EXP2_SCALE = math.log2(math.e) / math.sqrt(HEAD)
 MASKED = -1e30
+ONES = 16
 MESH = pl.DeviceIdType.MESH
 
 
@@ -143,9 +144,9 @@
     forwards = odd & (srv >= 2)
 
     def project_kv(turn, c):
-        kv[0, c, halves[turn]] = jnp.dot(
-            tok[halves[turn]], wkv[c], preferred_element_type=jnp.float32
-        ).astype(jnp.bfloat16)
+        both = jnp.dot(tok[halves[turn]], wkv[c], preferred_element_type=jnp.float32)
+        kv[0, c, halves[turn], :, :HEAD] = both[:, :HEAD].astype(jnp.bfloat16)
+        kv[0, c, halves[turn], :, HEAD:] = jnp.transpose(both[:, HEAD:]).astype(jnp.bfloat16)
 
         @pl.when(sends_two)
         def _():
@@ -196,49 +197,58 @@
         return jnp.transpose(jnp.broadcast_to(ids, (HEAD, HEAD)))
 
     def set_bias(block):
-        for r in range(2):
-            mine = column(r)
-            for s in range(2):
-                theirs = docs[2 * block + s].astype(jnp.float32)
-                allowed = mine == theirs
+        for s in range(2):
+            theirs = column(2 * block + s)
+            for r in range(2):
+                mine = docs[r].astype(jnp.float32)
+                allowed = theirs == mine
                 if block == 0:
-                    rows = lax.broadcasted_iota(jnp.int32, (HEAD, HEAD), 0) + r * HEAD
-                    cols = lax.broadcasted_iota(jnp.int32, (HEAD, HEAD), 1) + s * HEAD
-                    allowed = allowed & (cols <= rows)
-                bias[block, r * HEAD : (r + 1) * HEAD, s * HEAD : (s + 1) * HEAD] = jnp.where(allowed, 0.0, MASKED)
-
-    ones = jnp.ones((2 * tok_dev, HEAD), jnp.bfloat16)
+                    keys = lax.broadcasted_iota(jnp.int32, (HEAD, HEAD), 0) + s * HEAD
+                    queries = lax.broadcasted_iota(jnp.int32, (HEAD, HEAD), 1) + r * HEAD
+                    allowed = allowed & (keys <= queries)
+                bias[block, r, s * HEAD : (s + 1) * HEAD, :] = jnp.where(allowed, 0.0, MASKED)
+
+    first_key = {0: (0, 0), 1: (0, 0), 2: (0, tok_dev)}
+    last_key = {0: (tok_dev, 2 * tok_dev), 1: (2 * tok_dev,) * 2, 2: (2 * tok_dev,) * 2}
 
     def attend(block, c):
-        both = kv[block, c].reshape(2 * tok_dev, 2 * HEAD)
-        keys = both[:, :HEAD]
-        values = jnp.concatenate([both[:, HEAD:], ones], axis=1)
-
-        def scores(g):
-            return lax.dot_general(
-                q[c * REPEAT + g],
-                keys,
-                (((1,), (1,)), ((), ())),
-                preferred_element_type=jnp.float32,
-            )
-
-        ahead = scores(0)
+        keys = kv[block, c].reshape(2 * tok_dev, 2 * HEAD)[:, :HEAD]
+        values = jnp.concatenate([kv[block, c, 0, :, HEAD:], kv[block, c, 1, :, HEAD:]], axis=1)
+        values = jnp.concatenate([values, jnp.ones((ONES, 2 * tok_dev), jnp.bfloat16)], axis=0)
         for g in range(REPEAT):
             h = c * REPEAT + g
-            score = ahead + bias[block]
-            if g + 1 < REPEAT:
-                ahead = scores(g + 1)
-            high = jnp.max(score, axis=1, keepdims=True)
-            if block:
-                before = top[h][:, :1]
-                high = jnp.maximum(high, before)
-            weight = jnp.exp2((score - high) * EXP2_SCALE).astype(jnp.bfloat16)
-            part = jnp.dot(weight, values, preferred_element_type=jnp.float32)
-            if block:
-                part = part + acc[h] * jnp.exp2((before - high) * EXP2_SCALE)
-            acc[h] = part
-            if block != 1:
-                top[h] = jnp.broadcast_to(high, (2 * tok_dev, HEAD))
+            for r in range(2):
+                lo, hi = first_key[block][r], last_key[block][r]
+                score = lax.dot_general(
+                    keys[lo:hi],
+                    q[h, r * tok_dev : (r + 1) * tok_dev],
+                    (((1,), (1,)), ((), ())),
+                    preferred_element_type=jnp.float32,
+                )
+                score = score + bias[block, r, lo:hi]
+                high = jnp.max(score, axis=0, keepdims=True)
+                if block:
+                    before = top[h, r]
+                    high = jnp.maximum(high, before)
+                weight = jnp.exp2((score - high) * EXP2_SCALE).astype(jnp.bfloat16)
+                part = jnp.dot(values[:, lo:hi], weight, preferred_element_type=jnp.float32)
+                if block:
+                    part = part + acc[h, r] * jnp.exp2((before - high) * EXP2_SCALE)
+                acc[h, r] = part
+                if block != 1:
+                    top[h, r] = high
+
+    identity = (
+        lax.broadcasted_iota(jnp.int32, (tok_dev, tok_dev), 0)
+        == lax.broadcasted_iota(jnp.int32, (tok_dev, tok_dev), 1)
+    ).astype(jnp.bfloat16)
+
+    def result(h, half):
+        total = acc[h, half, HEAD : HEAD + 1]
+        rounded = (acc[h, half, :HEAD] * (1.0 / total)).astype(jnp.bfloat16)
+        return lax.dot_general(
+            identity, rounded, (((1,), (1,)), ((), ())), preferred_element_type=jnp.float32
+        ).astype(jnp.bfloat16)
 
     set_bias(0)
     for c in range(kv_heads):
@@ -285,16 +295,12 @@
 
         for g in range(REPEAT):
             h = c * REPEAT + g
-            theirs = acc[h, pl.ds(pl.multiple_of(other * tok_dev, tok_dev), tok_dev)]
-            stage[c, :, g * HEAD : (g + 1) * HEAD] = (theirs[:, :HEAD] / theirs[:, HEAD:]).astype(
-                jnp.bfloat16
-            )
+            stage[c, :, g * HEAD : (g + 1) * HEAD] = result(h, other)
         out_copy(c).start()
         for g in range(REPEAT):
             h = c * REPEAT + g
-            mine = acc[h, pl.ds(pl.multiple_of(head * tok_dev, tok_dev), tok_dev)]
             at = pl.multiple_of((head * kv_heads + c) * REPEAT * HEAD + g * HEAD, HEAD)
-            out_ref[:, pl.ds(at, HEAD)] = (mine[:, :HEAD] / mine[:, HEAD:]).astype(jnp.bfloat16)
+            out_ref[:, pl.ds(at, HEAD)] = result(h, head)
 
     pair_tok.wait_send()
     pair_doc.wait_send()
@@ -341,9 +347,9 @@
             pltpu.VMEM((q_blocks, width, 2 * HEAD), bf16),
             pltpu.VMEM((3, kv_heads, 2, tok_dev, 2 * HEAD), bf16),
             pltpu.VMEM((heads, 2 * tok_dev, HEAD), bf16),
-            pltpu.VMEM((heads, 2 * tok_dev, 2 * HEAD), f32),
-            pltpu.VMEM((heads, 2 * tok_dev, HEAD), f32),
-            pltpu.VMEM((3, 2 * tok_dev, 2 * tok_dev), f32),
+            pltpu.VMEM((heads, 2, HEAD + ONES, tok_dev), f32),
+            pltpu.VMEM((heads, 2, 1, tok_dev), f32),
+            pltpu.VMEM((3, 2, 2 * tok_dev, tok_dev), f32),
             pltpu.VMEM((6, 1, tok_dev), jnp.int32),
             pltpu.VMEM((kv_heads, tok_dev, REPEAT * HEAD), bf16),
             dma,
@@ -360,7 +366,7 @@
             dma((kv_heads,)),
         ],
         compiler_params=pltpu.CompilerParams(
-            collective_id=0, has_side_effects=True, vmem_limit_bytes=56 * 1024 * 1024
+            collective_id=0, has_side_effects=True, vmem_limit_bytes=53 * 1024 * 1024
         ),
     )(tokens, doc_ids.reshape(1, tok_dev), w_query, w_key, value_weight)
 

time: 26.8 us -> 23.6 us (0.88)
  Pallas kernels: 24.6 us -> 22 us
  local copies, waits for them, and re-layouts: 1.88 us -> 1.45 us
    pallas_call x1, Pallas kernels: 24.6 us -> 22 us  [on_device(): pl.pallas_call(functools.partial(kernel, n), out_shape=jax.ShapeDtypeStru...]
    unnamed x1 -> x3, local copies, waits for them, and re-layouts: 1.88 us -> 1.45 us
where the time goes in v3:
time: 23.6 us; the launch traced here: 23.5 us
  Pallas kernels  22 us (93%)
  local copies, waits for them, and re-layouts  1.45 us (6%)
    pallas_call x1, Pallas kernels, on_device(): pl.pallas_call(functools.partial(kernel, n), out_shape=jax.ShapeDtypeStru...  22 us
    unnamed x3, local copies, waits for them, and re-layouts  1.45 us

profile of v3, /device:TPU:17, one launch (start us, length us, event | category | flops | bytes accessed | tf_op | source)
XLA Modules:
  0.0 23.5 jit_solution(12972907706537434727)
XLA Ops:
  0.0 0.0 copy-start
  0.0 0.7 %copy-done = s32[128]{0:T(128)S(1)} copy-done((s32[128]{0:T(128)S(1)}, s32[128]{0:T(128)}, u32[]{:S(2)}) %copy-start) | copy-done | bytes 536
  0.7 22.0 %shard_map.55 = bf16[128,2048]{1,0:T(8,128)(2,1)S(1)} custom-call(bf16[128,4096]{1,0:T(8,128)(2,1)} %tok_hbm.1, s32[1,128]{1,0:T(1,128)S(1)} %bitcast.1, bf16[4096,1024]{1,0:T(8,128)(2,1)} %wq_hbm.1, bf16[4096,256]{1,0:T(8,128)(2,1)} %wk_hbm.1, bf16[4096,256]{1,0:T(8,128)(2,1)} %wv_hbm.1), custom_call_target="tpu_custom_call" | custom-call | tf_op jit(solution)/shard_map/pallas_call | solution.py:339
  22.7 0.8 %copy.7 = bf16[128,2048]{1,0:T(8,128)(2,1)} copy(bf16[128,2048]{1,0:T(8,128)(2,1)S(1)} %shard_map.55) | data formatting | bytes 1048576
Async XLA Ops:
  0.0 0.7 %copy-start = (s32[128]{0:T(128)S(1)}, s32[128]{0:T(128)}, u32[]{:S(2)}) copy-start(s32[128]{0:T(128)} %param.6) | copy-start | bytes 1540

commit v4 on v3

--- a/solution.py
+++ b/solution.py
@@ -13,6 +13,7 @@
 EXP2_SCALE = math.log2(math.e) / math.sqrt(HEAD)
 MASKED = -1e30
 ONES = 16
+ROW_BLOCKS = 4
 MESH = pl.DeviceIdType.MESH
 
 
@@ -29,6 +30,7 @@
     wq,
     kv,
     q,
+    q_sum,
     acc,
     top,
     bias,
@@ -51,8 +53,8 @@
     head = lax.axis_index("head")
     other = 1 - head
     tok_dev = tok.shape[1]
-    kv_heads = wkv.shape[0]
-    q_blocks = wq.shape[0]
+    kv_heads = wkv.shape[2] // HEAD
+    q_blocks = wq.shape[2] // 256
     even = srv % 2 == 0
     odd = srv % 2 == 1
 
@@ -61,24 +63,18 @@
 
     own_tok = local(tok_hbm, tok.at[head], tok_sem)
     own_doc = local(doc_hbm, docs.at[head], doc_sem)
-    wkv_copies = []
-    for c in range(kv_heads):
-        cols = pl.ds(c * HEAD, HEAD)
-        wkv_copies.append(
-            (
-                local(wk_hbm.at[:, cols], wkv.at[c, :, pl.ds(0, HEAD)], wkv_sem.at[c, 0]),
-                local(wv_hbm.at[:, cols], wkv.at[c, :, pl.ds(HEAD, HEAD)], wkv_sem.at[c, 1]),
-            )
-        )
+    wkv_copies = (
+        local(wk_hbm, wkv.at[0], wkv_sem.at[0]),
+        local(wv_hbm, wkv.at[1], wkv_sem.at[1]),
+    )
+    depth = wq.shape[1]
     wq_copies = [
-        local(wq_hbm.at[:, pl.ds(j * 256, 256)], wq.at[j], wq_sem.at[j]) for j in range(q_blocks)
+        local(wq_hbm.at[pl.ds(j * depth, depth)], wq.at[j], wq_sem.at[j])
+        for j in range(wq.shape[0])
     ]
     own_tok.start()
     own_doc.start()
-    for pair in wkv_copies:
-        for copy in pair:
-            copy.start()
-    for copy in wq_copies:
+    for copy in wkv_copies:
         copy.start()
 
     barrier = pltpu.get_barrier_semaphore()
@@ -109,6 +105,8 @@
     pair_doc = remote(doc_hbm, docs.at[head], pair_send.at[1], pair_recv.at[1], partner)
     pair_doc.start()
     pair_tok.start()
+    for copy in wq_copies:
+        copy.start()
 
     def doc_copy(by):
         return remote(
@@ -143,25 +141,40 @@
     sends_two = srv + 2 < n
     forwards = odd & (srv >= 2)
 
-    def project_kv(turn, c):
-        both = jnp.dot(tok[halves[turn]], wkv[c], preferred_element_type=jnp.float32)
-        kv[0, c, halves[turn], :, :HEAD] = both[:, :HEAD].astype(jnp.bfloat16)
-        kv[0, c, halves[turn], :, HEAD:] = jnp.transpose(both[:, HEAD:]).astype(jnp.bfloat16)
-
-        @pl.when(sends_two)
-        def _():
-            kv_copy(2, turn, c).start()
-
-        @pl.when(sends_one)
-        def _():
-            kv_copy(1, turn, c).start()
-
-    def project_q(j):
-        block = jnp.dot(
-            tok[...].reshape(2 * tok_dev, tok.shape[2]), wq[j], preferred_element_type=jnp.float32
-        ).astype(jnp.bfloat16)
-        q[2 * j] = block[:, :HEAD]
-        q[2 * j + 1] = block[:, HEAD:]
+    def project_kv(turn, first):
+        half = halves[turn]
+        if first:
+            wkv_copies[0].wait()
+        keys = jnp.dot(tok[half], wkv[0], preferred_element_type=jnp.float32)
+        if first:
+            wkv_copies[1].wait()
+        values = jnp.dot(tok[half], wkv[1], preferred_element_type=jnp.float32)
+        for c in range(kv_heads):
+            cols = slice(c * HEAD, (c + 1) * HEAD)
+            kv[0, c, half, :, :HEAD] = keys[:, cols].astype(jnp.bfloat16)
+            kv[0, c, half, :, HEAD:] = jnp.transpose(values[:, cols]).astype(jnp.bfloat16)
+
+            @pl.when(sends_two)
+            def _():
+                kv_copy(2, turn, c).start()
+
+            @pl.when(sends_one)
+            def _():
+                kv_copy(1, turn, c).start()
+
+    def project_q(block):
+        rows = tok[:, :, block * depth : (block + 1) * depth].reshape(2 * tok_dev, depth)
+        for j in range(q_blocks):
+            part = jnp.dot(
+                rows, wq[block, :, j * 256 : (j + 1) * 256], preferred_element_type=jnp.float32
+            )
+            if block:
+                part = part + q_sum[j]
+            if block + 1 < len(wq_copies):
+                q_sum[j] = part
+            else:
+                q[2 * j] = part[:, :HEAD].astype(jnp.bfloat16)
+                q[2 * j + 1] = part[:, HEAD:].astype(jnp.bfloat16)
 
     def forward(turn, c):
         @pl.when(forwards)
@@ -171,10 +184,7 @@
 
     own_tok.wait()
     own_doc.wait()
-    for c in range(kv_heads):
-        for copy in wkv_copies[c]:
-            copy.wait()
-        project_kv(0, c)
+    project_kv(0, True)
     pair_doc.wait_recv()
     for by in (1, 2):
 
@@ -183,14 +193,13 @@
             doc_copy(by).start()
 
     pair_tok.wait_recv()
-    for c in range(kv_heads):
-        project_kv(1, c)
-    for j in range(q_blocks):
-        if j == q_blocks // 2:
+    project_kv(1, False)
+    for block in range(len(wq_copies)):
+        if block == 2:
             for c in range(kv_heads):
                 forward(0, c)
-        wq_copies[j].wait()
-        project_q(j)
+        wq_copies[block].wait()
+        project_q(block)
 
     def column(part):
         ids = docs[part].astype(jnp.float32)
@@ -343,18 +352,19 @@
         out_specs=pl.BlockSpec(memory_space=pltpu.VMEM),
         scratch_shapes=[
             pltpu.VMEM((2, tok_dev, width), bf16),
-            pltpu.VMEM((kv_heads, width, 2 * HEAD), bf16),
-            pltpu.VMEM((q_blocks, width, 2 * HEAD), bf16),
+            pltpu.VMEM((2, width, kv_heads * HEAD), bf16),
+            pltpu.VMEM((ROW_BLOCKS, width // ROW_BLOCKS, heads * HEAD), bf16),
             pltpu.VMEM((3, kv_heads, 2, tok_dev, 2 * HEAD), bf16),
             pltpu.VMEM((heads, 2 * tok_dev, HEAD), bf16),
+            pltpu.VMEM((q_blocks, 2 * tok_dev, 256), f32),
             pltpu.VMEM((heads, 2, HEAD + ONES, tok_dev), f32),
             pltpu.VMEM((heads, 2, 1, tok_dev), f32),
             pltpu.VMEM((3, 2, 2 * tok_dev, tok_dev), f32),
             pltpu.VMEM((6, 1, tok_dev), jnp.int32),
             pltpu.VMEM((kv_heads, tok_dev, REPEAT * HEAD), bf16),
             dma,
-            dma((kv_heads, 2)),
-            dma((q_blocks,)),
+            dma((2,)),
+            dma((ROW_BLOCKS,)),
             dma,
             dma((2,)),
             dma((2,)),

time: 23.6 us -> 22.1 us (0.936)
  Pallas kernels: 22 us -> 20.5 us
    pallas_call x1, Pallas kernels: 22 us -> 20.5 us  [on_device(): pl.pallas_call(functools.partial(kernel, n), out_shape=jax.ShapeDtypeStru...]
where the time goes in v4:
time: 22.1 us; the launch traced here: 21.9 us
  Pallas kernels  20.5 us (93%)
  local copies, waits for them, and re-layouts  1.45 us (7%)
    pallas_call x1, Pallas kernels, on_device(): pl.pallas_call(functools.partial(kernel, n), out_shape=jax.ShapeDtypeStru...  20.5 us
    unnamed x3, local copies, waits for them, and re-layouts  1.45 us

profile of v4, /device:TPU:17, one launch (start us, length us, event | category | flops | bytes accessed | tf_op | source)
XLA Modules:
  0.0 21.9 jit_solution(14639959157819914589)
XLA Ops:
  0.0 0.0 copy-start
  0.0 0.7 %copy-done = s32[128]{0:T(128)S(1)} copy-done((s32[128]{0:T(128)S(1)}, s32[128]{0:T(128)}, u32[]{:S(2)}) %copy-start) | copy-done | bytes 536
  0.7 20.5 %shard_map.55 = bf16[128,2048]{1,0:T(8,128)(2,1)S(1)} custom-call(bf16[128,4096]{1,0:T(8,128)(2,1)} %tok_hbm.1, s32[1,128]{1,0:T(1,128)S(1)} %bitcast.1, bf16[4096,1024]{1,0:T(8,128)(2,1)} %wq_hbm.1, bf16[4096,256]{1,0:T(8,128)(2,1)} %wk_hbm.1, bf16[4096,256]{1,0:T(8,128)(2,1)} %wv_hbm.1), custom_call_target="tpu_custom_call" | custom-call | tf_op jit(solution)/shard_map/pallas_call | solution.py:348
  21.2 0.8 %copy.7 = bf16[128,2048]{1,0:T(8,128)(2,1)} copy(bf16[128,2048]{1,0:T(8,128)(2,1)S(1)} %shard_map.55) | data formatting | bytes 1048576
Async XLA Ops:
  0.0 0.7 %copy-start = (s32[128]{0:T(128)S(1)}, s32[128]{0:T(128)}, u32[]{:S(2)}) copy-start(s32[128]{0:T(128)} %param.6) | copy-start | bytes 1540

commit v5 on v4

--- a/solution.py
+++ b/solution.py
@@ -195,11 +195,10 @@
     pair_tok.wait_recv()
     project_kv(1, False)
     for block in range(len(wq_copies)):
-        if block == 2:
-            for c in range(kv_heads):
-                forward(0, c)
         wq_copies[block].wait()
         project_q(block)
+    for c in range(kv_heads):
+        forward(0, c)
 
     def column(part):
         ids = docs[part].astype(jnp.float32)

time: 22.1 us -> 21.1 us (0.955)
  Pallas kernels: 20.5 us -> 19.5 us
    pallas_call x1, Pallas kernels: 20.5 us -> 19.5 us  [on_device(): pl.pallas_call(functools.partial(kernel, n), out_shape=jax.ShapeDtypeStru...]
where the time goes in v5:
time: 21.1 us; the launch traced here: 21 us
  Pallas kernels  19.5 us (92%)
  local copies, waits for them, and re-layouts  1.45 us (7%)
    pallas_call x1, Pallas kernels, on_device(): pl.pallas_call(functools.partial(kernel, n), out_shape=jax.ShapeDtypeStru...  19.5 us
    unnamed x3, local copies, waits for them, and re-layouts  1.45 us

profile of v5, /device:TPU:17, one launch (start us, length us, event | category | flops | bytes accessed | tf_op | source)
XLA Modules:
  0.0 21.0 jit_solution(5517970424954362255)
XLA Ops:
  0.0 0.0 copy-start
  0.0 0.7 %copy-done = s32[128]{0:T(128)S(1)} copy-done((s32[128]{0:T(128)S(1)}, s32[128]{0:T(128)}, u32[]{:S(2)}) %copy-start) | copy-done | bytes 536
  0.7 19.5 %shard_map.55 = bf16[128,2048]{1,0:T(8,128)(2,1)S(1)} custom-call(bf16[128,4096]{1,0:T(8,128)(2,1)} %tok_hbm.1, s32[1,128]{1,0:T(1,128)S(1)} %bitcast.1, bf16[4096,1024]{1,0:T(8,128)(2,1)} %wq_hbm.1, bf16[4096,256]{1,0:T(8,128)(2,1)} %wk_hbm.1, bf16[4096,256]{1,0:T(8,128)(2,1)} %wv_hbm.1), custom_call_target="tpu_custom_call" | custom-call | tf_op jit(solution)/shard_map/pallas_call | solution.py:347
  20.2 0.8 %copy.7 = bf16[128,2048]{1,0:T(8,128)(2,1)} copy(bf16[128,2048]{1,0:T(8,128)(2,1)S(1)} %shard_map.55) | data formatting | bytes 1048576
Async XLA Ops:
  0.0 0.7 %copy-start = (s32[128]{0:T(128)S(1)}, s32[128]{0:T(128)}, u32[]{:S(2)}) copy-start(s32[128]{0:T(128)} %param.6) | copy-start | bytes 1540

commit v6 on v5

--- a/solution.py
+++ b/solution.py
@@ -14,6 +14,7 @@
 MASKED = -1e30
 ONES = 16
 ROW_BLOCKS = 4
+TOK_PIECES = 4
 MESH = pl.DeviceIdType.MESH
 
 
@@ -101,10 +102,16 @@
         )
 
     partner = (srv, other)
-    pair_tok = remote(tok_hbm, tok.at[head], pair_send.at[0], pair_recv.at[0], partner)
-    pair_doc = remote(doc_hbm, docs.at[head], pair_send.at[1], pair_recv.at[1], partner)
+    piece = tok_dev // TOK_PIECES
+    pair_tok = []
+    for p in range(TOK_PIECES):
+        rows = tok.at[head, pl.ds(p * piece, piece)]
+        pair_tok.append(remote(rows, rows, pair_send.at[1 + p], pair_recv.at[1 + p], partner))
+    pair_doc = remote(doc_hbm, docs.at[head], pair_send.at[0], pair_recv.at[0], partner)
     pair_doc.start()
-    pair_tok.start()
+    own_tok.wait()
+    for copy in pair_tok:
+        copy.start()
     for copy in wq_copies:
         copy.start()
 
@@ -182,7 +189,6 @@
             kv_copy(2, turn, c).wait_recv()
             kv_forward(turn, c).start()
 
-    own_tok.wait()
     own_doc.wait()
     project_kv(0, True)
     pair_doc.wait_recv()
@@ -192,7 +198,8 @@
         def _(by=by):
             doc_copy(by).start()
 
-    pair_tok.wait_recv()
+    for copy in pair_tok:
+        copy.wait_recv()
     project_kv(1, False)
     for block in range(len(wq_copies)):
         wq_copies[block].wait()
@@ -310,7 +317,8 @@
             at = pl.multiple_of((head * kv_heads + c) * REPEAT * HEAD + g * HEAD, HEAD)
             out_ref[:, pl.ds(at, HEAD)] = result(h, head)
 
-    pair_tok.wait_send()
+    for copy in pair_tok:
+        copy.wait_send()
     pair_doc.wait_send()
     for by in (1, 2):
 
@@ -365,8 +373,8 @@
             dma((2,)),
             dma((ROW_BLOCKS,)),
             dma,
-            dma((2,)),
-            dma((2,)),
+            dma((1 + TOK_PIECES,)),
+            dma((1 + TOK_PIECES,)),
             dma((2,)),
             dma((2,)),
             dma((2, 2, kv_heads)),

time: 21.1 us -> 21 us (level)
  no operation moved by 1% of the time
where the time goes in v6:
time: 21 us; the launch traced here: 20.8 us
  Pallas kernels  19.4 us (92%)
  local copies, waits for them, and re-layouts  1.45 us (7%)
    pallas_call x1, Pallas kernels, on_device(): pl.pallas_call(functools.partial(kernel, n), out_shape=jax.ShapeDtypeStru...  19.4 us
    unnamed x3, local copies, waits for them, and re-layouts  1.45 us

profile of v6, /device:TPU:17, one launch (start us, length us, event | category | flops | bytes accessed | tf_op | source)
XLA Modules:
  0.0 20.8 jit_solution(1923327871696229098)
XLA Ops:
  0.0 0.0 copy-start
  0.0 0.7 %copy-done = s32[128]{0:T(128)S(1)} copy-done((s32[128]{0:T(128)S(1)}, s32[128]{0:T(128)}, u32[]{:S(2)}) %copy-start) | copy-done | bytes 536
  0.7 19.4 %shard_map.55 = bf16[128,2048]{1,0:T(8,128)(2,1)S(1)} custom-call(bf16[128,4096]{1,0:T(8,128)(2,1)} %tok_hbm.1, s32[1,128]{1,0:T(1,128)S(1)} %bitcast.1, bf16[4096,1024]{1,0:T(8,128)(2,1)} %wq_hbm.1, bf16[4096,256]{1,0:T(8,128)(2,1)} %wk_hbm.1, bf16[4096,256]{1,0:T(8,128)(2,1)} %wv_hbm.1), custom_call_target="tpu_custom_call" | custom-call | tf_op jit(solution)/shard_map/pallas_call | solution.py:355
  20.1 0.8 %copy.7 = bf16[128,2048]{1,0:T(8,128)(2,1)} copy(bf16[128,2048]{1,0:T(8,128)(2,1)S(1)} %shard_map.55) | data formatting | bytes 1048576
Async XLA Ops:
  0.0 0.7 %copy-start = (s32[128]{0:T(128)S(1)}, s32[128]{0:T(128)}, u32[]{:S(2)}) copy-start(s32[128]{0:T(128)} %param.6) | copy-start | bytes 1540

commit v7 on v6

--- a/solution.py
+++ b/solution.py
@@ -148,6 +148,12 @@
     sends_two = srv + 2 < n
     forwards = odd & (srv >= 2)
 
+    def relayed(turn, c):
+        return (turn, c) != (1, kv_heads - 1)
+
+    def sends_next(turn, c):
+        return sends_one if relayed(turn, c) else srv + 1 < n
+
     def project_kv(turn, first):
         half = halves[turn]
         if first:
@@ -165,7 +171,7 @@
             def _():
                 kv_copy(2, turn, c).start()
 
-            @pl.when(sends_one)
+            @pl.when(sends_next(turn, c))
             def _():
                 kv_copy(1, turn, c).start()
 
@@ -184,6 +190,9 @@
                 q[2 * j + 1] = part[:, HEAD:].astype(jnp.bfloat16)
 
     def forward(turn, c):
+        if not relayed(turn, c):
+            return
+
         @pl.when(forwards)
         def _():
             kv_copy(2, turn, c).wait_recv()
@@ -277,9 +286,10 @@
         set_bias(2)
         for c in range(kv_heads):
 
-            @pl.when(even)
-            def _():
-                for turn in range(2):
+            for turn in range(2):
+
+                @pl.when(even if relayed(turn, c) else srv >= 2)
+                def _():
                     kv_copy(2, turn, c).wait_recv()
 
             attend(2, c)
@@ -333,13 +343,15 @@
             def _():
                 kv_copy(2, turn, c).wait_send()
 
-            @pl.when(sends_one)
+            @pl.when(sends_next(turn, c))
             def _():
                 kv_copy(1, turn, c).wait_send()
 
-            @pl.when(forwards)
-            def _():
-                kv_forward(turn, c).wait_send()
+            if relayed(turn, c):
+
+                @pl.when(forwards)
+                def _():
+                    kv_forward(turn, c).wait_send()
 
     for c in range(kv_heads):
         out_copy(c).wait()

time: 21 us -> 21.7 us (1.033)
  the two profiles are of different devices: /device:TPU:17 before, /device:TPU:21 now
where the time goes in v7:
time: 21.7 us; the launch traced here: 21.5 us
  Pallas kernels  20.1 us (93%)
  local copies, waits for them, and re-layouts  1.45 us (7%)
    pallas_call x1, Pallas kernels, on_device(): pl.pallas_call(functools.partial(kernel, n), out_shape=jax.ShapeDtypeStru...  20.1 us
    unnamed x3, local copies, waits for them, and re-layouts  1.45 us

profile of v7, /device:TPU:21, one launch (start us, length us, event | category | flops | bytes accessed | tf_op | source)
XLA Modules:
  0.0 21.5 jit_solution(6387869317445374864)
XLA Ops:
  0.0 0.0 copy-start
  0.0 0.7 %copy-done = s32[128]{0:T(128)S(1)} copy-done((s32[128]{0:T(128)S(1)}, s32[128]{0:T(128)}, u32[]{:S(2)}) %copy-start) | copy-done | bytes 536
  0.7 20.1 %shard_map.55 = bf16[128,2048]{1,0:T(8,128)(2,1)S(1)} custom-call(bf16[128,4096]{1,0:T(8,128)(2,1)} %tok_hbm.1, s32[1,128]{1,0:T(1,128)S(1)} %bitcast.1, bf16[4096,1024]{1,0:T(8,128)(2,1)} %wq_hbm.1, bf16[4096,256]{1,0:T(8,128)(2,1)} %wk_hbm.1, bf16[4096,256]{1,0:T(8,128)(2,1)} %wv_hbm.1), custom_call_target="tpu_custom_call" | custom-call | tf_op jit(solution)/shard_map/pallas_call | solution.py:367
  20.7 0.8 %copy.7 = bf16[128,2048]{1,0:T(8,128)(2,1)} copy(bf16[128,2048]{1,0:T(8,128)(2,1)S(1)} %shard_map.55) | data formatting | bytes 1048576
Async XLA Ops:
  0.0 0.7 %copy-start = (s32[128]{0:T(128)S(1)}, s32[128]{0:T(128)}, u32[]{:S(2)}) copy-start(s32[128]{0:T(128)} %param.6) | copy-start | bytes 1540

commit v8 on v6

--- a/solution.py
+++ b/solution.py
@@ -161,7 +161,7 @@
             kv[0, c, half, :, :HEAD] = keys[:, cols].astype(jnp.bfloat16)
             kv[0, c, half, :, HEAD:] = jnp.transpose(values[:, cols]).astype(jnp.bfloat16)
 
-            @pl.when(sends_two)
+            @pl.when(sends_two & even if turn else sends_two)
             def _():
                 kv_copy(2, turn, c).start()
 
@@ -204,6 +204,12 @@
     for block in range(len(wq_copies)):
         wq_copies[block].wait()
         project_q(block)
+        if block % 2 == 0 and block // 2 < kv_heads:
+
+            @pl.when(sends_two & odd)
+            def _():
+                kv_copy(2, 1, block // 2).start()
+
     for c in range(kv_heads):
         forward(0, c)
 

time: 21 us -> 21 us (level)
  no operation moved by 1% of the time
where the time goes in v8:
time: 21 us; the launch traced here: 20.8 us
  Pallas kernels  19.4 us (92%)
  local copies, waits for them, and re-layouts  1.45 us (7%)
    pallas_call x1, Pallas kernels, on_device(): pl.pallas_call(functools.partial(kernel, n), out_shape=jax.ShapeDtypeStru...  19.4 us
    unnamed x3, local copies, waits for them, and re-layouts  1.45 us

profile of v8, /device:TPU:17, one launch (start us, length us, event | category | flops | bytes accessed | tf_op | source)
XLA Modules:
  0.0 20.8 jit_solution(5287854257603050703)
XLA Ops:
  0.0 0.0 copy-start
  0.0 0.7 %copy-done = s32[128]{0:T(128)S(1)} copy-done((s32[128]{0:T(128)S(1)}, s32[128]{0:T(128)}, u32[]{:S(2)}) %copy-start) | copy-done | bytes 536
  0.7 19.4 %shard_map.55 = bf16[128,2048]{1,0:T(8,128)(2,1)S(1)} custom-call(bf16[128,4096]{1,0:T(8,128)(2,1)} %tok_hbm.1, s32[1,128]{1,0:T(1,128)S(1)} %bitcast.1, bf16[4096,1024]{1,0:T(8,128)(2,1)} %wq_hbm.1, bf16[4096,256]{1,0:T(8,128)(2,1)} %wk_hbm.1, bf16[4096,256]{1,0:T(8,128)(2,1)} %wv_hbm.1), custom_call_target="tpu_custom_call" | custom-call | tf_op jit(solution)/shard_map/pallas_call | solution.py:361
  20.0 0.8 %copy.7 = bf16[128,2048]{1,0:T(8,128)(2,1)} copy(bf16[128,2048]{1,0:T(8,128)(2,1)S(1)} %shard_map.55) | data formatting | bytes 1048576
Async XLA Ops:
  0.0 0.7 %copy-start = (s32[128]{0:T(128)S(1)}, s32[128]{0:T(128)}, u32[]{:S(2)}) copy-start(s32[128]{0:T(128)} %param.6) | copy-start | bytes 1540
